TPU v7x, 128 devices: a whole 4x4x4 slice. The times are simulated.
128 devices in a mesh: level: 4 (over x), grp: 32 (over z, y, core).
Axes of the slice: x: 4, y: 4, z: 4, core: 2. Of those that a mesh axis runs over, the one named last changes fastest.
Arguments:
- x_old: bfloat16 [4, 512, 16, 128], P('level', 'grp'), may hold values from -6 to 6
- rhs: float32 [4, 512, 16, 128], P('level', 'grp'), may hold values from -6 to 6
- down_tiles: bfloat16 [4, 512, 6, 128, 128], P('level', 'grp'), may hold values from -0.4375 to 0.4375
- level_tiles: bfloat16 [4, 512, 6, 128, 128], P('level', 'grp'), may hold values from -0.1875 to 0.1875
- up_tiles: bfloat16 [4, 512, 6, 128, 128], P('level', 'grp'), may hold values from -0.1875 to 0.1875
- inverses: float32 [4, 512, 128, 128], P('level', 'grp'), as said below
- tile_cols: int32 [4, 512, 3, 6], P('level', 'grp'), may hold values from 0 to 511
- tile_counts: int32 [4, 512, 3], P('level', 'grp'), may hold values from 1 to 6, as said below
Outputs:
- solution: float32 [4, 512, 16, 128], P('level', 'grp')
Inputs may be any that keep to these rules, and one draw needn't show every extreme that they name: `tile_counts`: slots at or beyond a block row's count are to be ignored; every level has a block row with 6 live slots in every band. `inverses`: each inverse is an arbitrary dense matrix given in full.
All inputs are finite; a program needn't handle non-finite values.
Results may differ from a plain program's by a relative error of at most 0.0015.
Values may be sent and summed in bfloat16 or wider, within the bound.
A program may use at most 64 MiB of HBM per device.

v0:
```python
import jax
import jax.numpy as jnp
from jax import lax
from jax.sharding import PartitionSpec as P


def from_behind(value, axis, by):
    length = lax.axis_size(axis)
    pairs = [(i, i + by) for i in range(length) if 0 <= i + by < length]
    return lax.ppermute(value, axis, pairs)


def band_term(tiles, cols, counts, source):
    pieces = source[cols]
    slots = jnp.arange(cols.shape[1], dtype=jnp.int32)
    live = slots[None, :] < counts[:, None]
    pieces = jnp.where(live[:, :, None, None], pieces, jnp.zeros((), pieces.dtype))
    return jnp.einsum("bkrc,bkcq->brq", pieces, tiles, preferred_element_type=jnp.float32)


def solve_blocks(resid, inverse):
    return jnp.einsum(
        "brc,bcq->brq",
        resid,
        inverse,
        precision=lax.Precision.HIGHEST,
        preferred_element_type=jnp.float32,
    )


def shards(x_old, rhs, down_tiles, level_tiles, up_tiles, inverses, tile_cols, tile_counts):
    own = x_old[0]
    whole = lax.all_gather(own, "grp", axis=0, tiled=True)
    above = from_behind(whole, "level", -1)
    cols = tile_cols[0]
    counts = tile_counts[0]
    base = rhs[0] - band_term(level_tiles[0], cols[:, 1], counts[:, 1], whole)
    base = base - band_term(up_tiles[0], cols[:, 2], counts[:, 2], above)
    inverse = inverses[0]
    down_here = down_tiles[0]
    first = solve_blocks(base, inverse)

    def level_turn(turn, current):
        outgoing = current.astype(jnp.bfloat16)
        gathered = lax.all_gather(outgoing, "grp", axis=0, tiled=True)
        panel = from_behind(gathered, "level", 1)
        resid = base - band_term(down_here, cols[:, 0], counts[:, 0], panel)
        return solve_blocks(resid, inverse)

    final = lax.fori_loop(1, lax.axis_size("level"), level_turn, first)
    return final[None]


def solution(mesh):
    return jax.shard_map(
        shards,
        mesh=mesh,
        in_specs=(
            P("level", "grp", None, None),
            P("level", "grp", None, None),
            P("level", "grp", None, None, None),
            P("level", "grp", None, None, None),
            P("level", "grp", None, None, None),
            P("level", "grp", None, None),
            P("level", "grp", None, None),
            P("level", "grp", None),
        ),
        out_specs=P("level", "grp", None, None),
        check_vma=False,
    )
```

profile of v0, /device:TPU:7, one launch (start us, length us, event | category | flops | bytes accessed | tf_op | source)
XLA Modules:
  0.0 424.9 jit_solution(5996172280538096552)
XLA Ops:
  6.5 0.7 all-gather.4.cloned.1.call-update
  7.3 49.1 %all-gather.4.cloned.1.call-done = bf16[1,512,16,128]{3,2,0,1:T(8,128)(2,1)} async-done(((bf16[1,16,16,128]{3,2,0,1:T(8,128)(2,1)}), bf16[1,512,16,128]{3,2,0,1:T(8,128)(2,1)}) %all-gather.4.cloned.1.call-update) | async-done | bytes 2097168 | tf_op jit(solution)/shard_map/all_gather | solution.py:33
  56.4 3.8 collective-permute-start.1
  60.2 1.3 copy.28
  61.5 0.8 compare_select_fusion.1
  62.3 0.1 copy.20
  62.4 0.1 reshape.160
  62.5 0.7 copy.29
  63.1 0.1 copy.21
  63.2 0.1 reshape.168
  63.4 0.4 copy-done.5
  63.7 0.1 iota_compare_fusion.1
  63.8 2.3 gather_fusion.1
  66.1 2.1 fusion.18
  68.2 35.7 %collective-permute-done.1 = bf16[512,16,128]{2,1,0:T(8,128)(2,1)} collective-permute-done((bf16[512,16,128]{2,1,0:T(8,128)(2,1)}, bf16[512,16,128]{2,1,0:T(8,128)(2,1)}, u32[]{:S(2)}, u32[]{:S(2)}) %collective-permute-start.1) | collective-permute-done | bytes 2097184 | tf_op jit(solution)/shard_map/ppermute | solution.py:10
  103.9 2.3 gather_fusion.2
  106.2 2.5 fusion.15
  108.8 1.0 fusion.27
  109.8 307.9 %while.10 = (s32[]{:T(128)}, f32[16,16,128]{2,1,0:T(8,128)S(1)}, s32[16,3]{0,1:T(4,128)}, s32[16,3,6]{0,1,2:T(4,128)}, bf16[16,6,128,128]{3,2,1,0:T(8,128)(2,1)}...) while((s32[]{:T(128)}, f32[16,16,128]{2,1,0:T(8,128)S(1)}, s32[16,3]{0,1:T(4,128)}, ...), condition=%wide.region_1.2_spmd, body=%wide.region_0.1_spmd.sunk | while | flops 100926848 | bytes 25173568 | solution.py:50
  109.8 0.0 all-gather.6.cloned.1.call-start
  109.8 0.6 convert_element_type.4
  110.5 0.1 all-gather.6.cloned.1.call-update
  110.5 48.1 %all-gather.6.cloned.1.call-done = bf16[512,16,128]{2,1,0:T(8,128)(2,1)} async-done(((bf16[16,16,128]{2,1,0:T(8,128)(2,1)}), bf16[512,16,128]{2,1,0:T(8,128)(2,1)}) %all-gather.6.cloned.1.call-update) | async-done | bytes 2097168 | tf_op jit(solution)/shard_map/while/body/eval_jaxpr/all_gather | solution.py:45
  158.6 1.3 collective-permute-start
  159.9 0.7 compare_select_fusion.4
  160.6 0.1 copy.31
  160.7 0.1 reshape.186
  160.8 0.7 slice_bitcast_fusion.6
  161.5 0.1 iota_compare_fusion.4
  161.5 46.2 %collective-permute-done = bf16[512,16,128]{2,1,0:T(8,128)(2,1)} collective-permute-done((bf16[512,16,128]{2,1,0:T(8,128)(2,1)}, bf16[512,16,128]{2,1,0:T(8,128)(2,1)}, u32[]{:S(2)}, u32[]{:S(2)}) %collective-permute-start) | collective-permute-done | bytes 2097184 | tf_op jit(solution)/shard_map/while/body/eval_jaxpr/ppermute | solution.py:10
  207.8 2.3 gather_fusion
  210.0 0.0 copy-start.2
  210.1 2.5 fusion.46
  212.6 1.0 fusion.47
  213.6 0.0 all-gather.6.cloned.1.call-start
  213.6 0.6 convert_element_type.4
  214.3 0.1 all-gather.6.cloned.1.call-update
  214.3 46.5 %all-gather.6.cloned.1.call-done = bf16[512,16,128]{2,1,0:T(8,128)(2,1)} async-done(((bf16[16,16,128]{2,1,0:T(8,128)(2,1)}), bf16[512,16,128]{2,1,0:T(8,128)(2,1)}) %all-gather.6.cloned.1.call-update) | async-done | bytes 2097168 | tf_op jit(solution)/shard_map/while/body/eval_jaxpr/all_gather | solution.py:45
  260.8 1.3 collective-permute-start
  262.1 0.7 compare_select_fusion.4
  262.8 0.1 copy.31
  262.9 0.1 reshape.186
  263.0 0.7 slice_bitcast_fusion.6
  263.6 0.1 iota_compare_fusion.4
  263.7 46.2 %collective-permute-done = bf16[512,16,128]{2,1,0:T(8,128)(2,1)} collective-permute-done((bf16[512,16,128]{2,1,0:T(8,128)(2,1)}, bf16[512,16,128]{2,1,0:T(8,128)(2,1)}, u32[]{:S(2)}, u32[]{:S(2)}) %collective-permute-start) | collective-permute-done | bytes 2097184 | tf_op jit(solution)/shard_map/while/body/eval_jaxpr/ppermute | solution.py:10
  310.0 2.3 gather_fusion
  312.2 2.5 fusion.46
  314.8 1.0 fusion.47
  315.8 0.0 all-gather.6.cloned.1.call-start
  315.8 0.6 convert_element_type.4
  316.5 0.0 all-gather.6.cloned.1.call-update
  316.5 46.2 %all-gather.6.cloned.1.call-done = bf16[512,16,128]{2,1,0:T(8,128)(2,1)} async-done(((bf16[16,16,128]{2,1,0:T(8,128)(2,1)}), bf16[512,16,128]{2,1,0:T(8,128)(2,1)}) %all-gather.6.cloned.1.call-update) | async-done | bytes 2097168 | tf_op jit(solution)/shard_map/while/body/eval_jaxpr/all_gather | solution.py:45
  362.7 1.3 collective-permute-start
  364.0 0.7 compare_select_fusion.4
  364.7 0.1 copy.31
  364.8 0.1 reshape.186
  364.9 0.7 slice_bitcast_fusion.6
  365.5 0.1 iota_compare_fusion.4
  365.6 46.2 %collective-permute-done = bf16[512,16,128]{2,1,0:T(8,128)(2,1)} collective-permute-done((bf16[512,16,128]{2,1,0:T(8,128)(2,1)}, bf16[512,16,128]{2,1,0:T(8,128)(2,1)}, u32[]{:S(2)}, u32[]{:S(2)}) %collective-permute-start) | collective-permute-done | bytes 2097184 | tf_op jit(solution)/shard_map/while/body/eval_jaxpr/ppermute | solution.py:10
  411.8 2.3 gather_fusion
  414.1 0.0 copy-start.2
  414.1 2.5 fusion.46
  416.7 1.0 fusion.47
  417.7 0.7 copy-done.4
  (19 shorter events, 0.1 us)
Async XLA Ops:
  6.5 59.5 %copy-start = (bf16[1,16,6,128,128]{4,3,2,1,0:T(8,128)(2,1)S(1)}, bf16[1,16,6,128,128]{4,3,2,1,0:T(8,128)(2,1)}, u32[]{:S(2)}) copy-start(bf16[1,16,6,128,128]{4,3,2,1,0:T(8,128)(2,1)} %param.13) | copy-start | bytes 9437188
  6.5 49.9 %all-gather.4.cloned.1.call-start = ((), (), s32[]{:S(2)}) async-start(), calls=%async_computation | async-start | bytes 2162688 | tf_op jit(solution)/shard_map/all_gather | solution.py:33
  56.4 47.6 %collective-permute-start.1 = (bf16[512,16,128]{2,1,0:T(8,128)(2,1)}, bf16[512,16,128]{2,1,0:T(8,128)(2,1)}, u32[]{:S(2)}, u32[]{:S(2)}) collective-permute-start(bf16[512,16,128]{2,1,0:T(8,128)(2,1)} %bitcast.92), channel_id=1, source_target_pairs={{32,0},{64,32},{96,64},{33,1},{65,33},{97,65},{34,2},{66,34},{98,6... | collective-permute-start | bytes 6291464 | tf_op jit(solution)/shard_map/ppermute | solution.py:10
  63.1 0.6 copy-start.5
  106.2 2.6 copy-start.1
  108.8 1.0 copy-start.3
  109.8 48.8 %all-gather.6.cloned.1.call-start = ((), (), s32[]{:S(2)}) async-start(), calls=%async_computation.1 | async-start | bytes 2162688 | tf_op jit(solution)/shard_map/while/body/eval_jaxpr/all_gather | solution.py:45
  158.6 49.2 %collective-permute-start = (bf16[512,16,128]{2,1,0:T(8,128)(2,1)}, bf16[512,16,128]{2,1,0:T(8,128)(2,1)}, u32[]{:S(2)}, u32[]{:S(2)}) collective-permute-start(bf16[512,16,128]{2,1,0:T(8,128)(2,1)} %all-gather.6.cloned.1.call-done), channel_id=1, source_target_pairs={{0,32},{32,64},{64,96},{1,33},{33,65},{65,97},{2,34},{34,66},{66,9... | collective-permute-start | bytes 6291464 | tf_op jit(solution)/shard_map/while/body/eval_jaxpr/ppermute | solution.py:10
  210.0 2.6 copy-start.2
  213.6 47.2 %all-gather.6.cloned.1.call-start = ((), (), s32[]{:S(2)}) async-start(), calls=%async_computation.1 | async-start | bytes 2162688 | tf_op jit(solution)/shard_map/while/body/eval_jaxpr/all_gather | solution.py:45
  260.8 49.2 %collective-permute-start = (bf16[512,16,128]{2,1,0:T(8,128)(2,1)}, bf16[512,16,128]{2,1,0:T(8,128)(2,1)}, u32[]{:S(2)}, u32[]{:S(2)}) collective-permute-start(bf16[512,16,128]{2,1,0:T(8,128)(2,1)} %all-gather.6.cloned.1.call-done), channel_id=1, source_target_pairs={{0,32},{32,64},{64,96},{1,33},{33,65},{65,97},{2,34},{34,66},{66,9... | collective-permute-start | bytes 6291464 | tf_op jit(solution)/shard_map/while/body/eval_jaxpr/ppermute | solution.py:10
  312.2 2.6 copy-start.2
  315.8 46.9 %all-gather.6.cloned.1.call-start = ((), (), s32[]{:S(2)}) async-start(), calls=%async_computation.1 | async-start | bytes 2162688 | tf_op jit(solution)/shard_map/while/body/eval_jaxpr/all_gather | solution.py:45
  362.7 49.2 %collective-permute-start = (bf16[512,16,128]{2,1,0:T(8,128)(2,1)}, bf16[512,16,128]{2,1,0:T(8,128)(2,1)}, u32[]{:S(2)}, u32[]{:S(2)}) collective-permute-start(bf16[512,16,128]{2,1,0:T(8,128)(2,1)} %all-gather.6.cloned.1.call-done), channel_id=1, source_target_pairs={{0,32},{32,64},{64,96},{1,33},{33,65},{65,97},{2,34},{34,66},{66,9... | collective-permute-start | bytes 6291464 | tf_op jit(solution)/shard_map/while/body/eval_jaxpr/ppermute | solution.py:10
  414.1 2.6 copy-start.2
  417.7 0.7 copy-start.4
Sparse Core Ops, SparseCore 0:
  9.6 46.7 all-gather.3
  112.9 45.6 all-gather.5
  216.7 44.0 all-gather.5
  318.6 44.0 all-gather.5
where the time goes:
time: 426 us; the launch traced here: 425 us
  waiting for transfers between devices  365 us (86%)
  local copies, waits for them, and re-layouts  17.2 us (4%)
  matrix products  16.3 us (4%)
  between operations  13.2 us (3%)
  starting transfers between devices  7.73 us (2%)
  other arithmetic  5.17 us (1%)
    ppermute x4, waiting for transfers between devices, from_behind(): return lax.ppermute(value, axis, pairs)  174 us
    all_gather x3, waiting for transfers between devices, level_turn(): gathered = lax.all_gather(outgoing, 'grp', axis=0, tiled=True)  141 us
    all_gather x1, waiting for transfers between devices, shards(): whole = lax.all_gather(own, 'grp', axis=0, tiled=True)  49.1 us
    dot_general x5, matrix products, band_term(): jnp.einsum('bkrc,bkcq->brq', pieces, tiles, preferred_element_type=jnp.fl...  12.3 us
    gather x5, local copies, waits for them, and re-layouts, band_term(): pieces = source[cols]  11.3 us
  transfers between devices with their start and end apart: 8, of which 8 were waited for; matrix products, arithmetic and copies ran while one was open for 3% of the time, Pallas kernels for 0%

commit v1 on v0

v1 whole, which is shorter than its diff:
```python
import functools

import jax
import jax.numpy as jnp
from jax import lax
from jax.experimental import pallas as pl
from jax.experimental.pallas import tpu as pltpu
from jax.sharding import PartitionSpec as P

MESH = pl.DeviceIdType.MESH
ROWS = 16
SLOTS = 6
TILE = 128
LEVELS = 4
PARTS = 2
WIDTH = ROWS // PARTS
SHARD = ROWS // PARTS
GROUP = 4 * SHARD
HALF = 16 * SHARD
OWN, ABOVE, DOWN = 1, 2, 0
F32, BF16 = jnp.float32, jnp.bfloat16


def fold(total):
    while total.shape[0] > WIDTH:
        half = total.shape[0] // 2
        total = total[:half] + total[half:]
    return total


def sweep(x_hbm, rhs_hbm, down_hbm, level_hbm, up_hbm, inv_hbm, cols, counts, out_hbm, *scratch):
    panels = {
        OWN: scratch[:PARTS],
        ABOVE: scratch[PARTS : 2 * PARTS],
        DOWN: scratch[2 * PARTS : 3 * PARTS],
    }
    outgoing = scratch[3 * PARTS : 4 * PARTS]
    results = scratch[4 * PARTS : 5 * PARTS]
    bases = scratch[5 * PARTS : 6 * PARTS]
    (x_vmem, rhs_vmem, down, level_t, up, inv, inv_split, masks, place, pick, load_sem, out_sem, send_sem, recv_sem) = scratch[6 * PARTS :]

    level = lax.axis_index("level")
    grp = lax.axis_index("grp")
    core = lax.rem(grp, 2)
    y = lax.rem(lax.div(grp, 2), 4)
    z = lax.div(grp, 8)
    first = core == 0
    a = jnp.where(first, y, z)
    b = jnp.where(first, z, y)
    lower = lax.rem(level + LEVELS - 1, LEVELS)
    upper = lax.rem(level + 1, LEVELS)

    def device(at_level, at_a, at_b):
        at_y = jnp.where(first, at_a, at_b)
        at_z = jnp.where(first, at_b, at_a)
        return (at_level, at_z * 8 + at_y * 2 + core)

    sibling = (level, z * 8 + y * 2 + 1 - core)

    def turn(value, by):
        return lax.rem(value + by, 4)

    loads = [
        (x_hbm.at[0], x_vmem),
        (level_hbm.at[0], level_t),
        (up_hbm.at[0], up),
        (rhs_hbm.at[0], rhs_vmem),
        (inv_hbm.at[0], inv),
        (down_hbm.at[0], down),
    ]
    loads = [pltpu.make_async_copy(src, dst, load_sem.at[n]) for n, (src, dst) in enumerate(loads)]
    for load in loads:
        load.start()

    barrier = pltpu.get_barrier_semaphore()
    partners = [sibling]
    partners += [device(level, turn(a, d), b) for d in (1, 2, 3)]
    partners += [device(level, a, turn(b, d)) for d in (1, 2, 3)]
    partners += [device(lower, turn(a, d), b) for d in (0, 1, 2, 3)]
    partners += [device(upper, turn(a, d), b) for d in (0, 1, 2, 3)]
    for partner in partners:
        pl.semaphore_signal(barrier, inc=1, device_id=partner, device_id_type=MESH)

    shard_at = (core * 16 + b * 4 + a) * SHARD
    shard = pl.ds(shard_at, SHARD)

    def group(at_core, at_b):
        return pl.ds((at_core * 16 + at_b * 4) * SHARD, GROUP)

    def half(at_core):
        return pl.ds(at_core * HALF, HALF)

    def recv(panel, part, which):
        return recv_sem.at[(panel * PARTS + part) * 5 + which]

    def sent(panel, part, which):
        return send_sem.at[(panel * PARTS + part) * 3 + which]

    def spread(source, panel, part, target, turns):
        for d in turns:
            pltpu.make_async_remote_copy(
                src_ref=source,
                dst_ref=panels[panel][part].at[shard],
                send_sem=sent(panel, part, 0),
                recv_sem=recv(panel, part, 0),
                device_id=device(target, turn(a, d), b),
                device_id_type=MESH,
            ).start()

    def wait_bytes(ref, sem):
        pltpu.make_async_copy(ref, ref, sem).wait()

    def to_sibling(panel, part, which):
        ref = panels[panel][part].at[which]
        pltpu.make_async_remote_copy(
            src_ref=ref,
            dst_ref=ref,
            send_sem=sent(panel, part, 2),
            recv_sem=recv(panel, part, 4),
            device_id=sibling,
            device_id_type=MESH,
        ).start()

    def relay(panel, part):
        ref = panels[panel][part]
        mine = ref.at[group(core, b)]
        if panel == OWN:
            wait_bytes(ref.at[pl.ds(0, 3 * SHARD)], recv(panel, part, 0))
        else:
            wait_bytes(mine, recv(panel, part, 0))
        for d in (2, 1, 3):
            pltpu.make_async_remote_copy(
                src_ref=mine,
                dst_ref=mine,
                send_sem=sent(panel, part, 1),
                recv_sem=recv(panel, part, d),
                device_id=device(level, a, turn(b, d)),
                device_id_type=MESH,
            ).start()
        to_sibling(panel, part, group(core, b))

    def share(panel, part):
        for d in (1, 3, 2):
            theirs = group(core, turn(b, 4 - d))
            wait_bytes(panels[panel][part].at[theirs], recv(panel, part, d))
            to_sibling(panel, part, theirs)

    def complete(panel, part):
        wait_bytes(panels[panel][part].at[half(1 - core)], recv(panel, part, 4))

    def drain(panel, part, shards):
        ref = panels[panel][part]
        wait_bytes(ref.at[pl.ds(0, shards * SHARD)], sent(panel, part, 0))

    def drain_rest(panel, part):
        ref = panels[panel][part]
        wait_bytes(ref.at[pl.ds(0, 3 * GROUP)], sent(panel, part, 1))
        wait_bytes(ref.at[pl.ds(0, 4 * GROUP)], sent(panel, part, 2))

    loads[0].wait()
    for part in range(PARTS):
        for j in range(SHARD):
            rows = [
                x_vmem[PARTS * j + q].astype(F32)[part * WIDTH : (part + 1) * WIDTH]
                for q in range(PARTS)
            ]
            panels[OWN][part][shard_at + j] = jnp.concatenate(rows, axis=0).astype(BF16)

    pl.semaphore_wait(barrier, len(partners))
    for part in range(PARTS):
        mine = panels[OWN][part].at[shard]
        spread(mine, OWN, part, level, (2, 1, 3))
        spread(mine, ABOVE, part, lower, (2, 1, 3, 0))

    row_group = lax.broadcasted_iota(jnp.int32, (ROWS, TILE), 0) // WIDTH
    for q in range(PARTS + 1):
        masks[q] = jnp.where(row_group == q, 1.0, 0.0).astype(BF16)

    def index_row(i, carry):
        for band in range(3):
            count = counts[0, i, band]
            if band == ABOVE:
                count = jnp.where(level == LEVELS - 1, 0, count)
            for k in range(SLOTS):
                col = cols[0, i, band, k]
                owner, j = lax.shift_right_logical(col, 4), lax.bitwise_and(col, 15)
                oz = lax.shift_right_logical(owner, 3)
                oy = lax.bitwise_and(lax.shift_right_logical(owner, 1), 3)
                even = lax.bitwise_and(owner, 1) == 0
                pos = jnp.where(even, oz * 4 + oy, 16 + oy * 4 + oz)
                place[band, i * SLOTS + k] = pos * SHARD + j // PARTS
                pick[band, i * SLOTS + k] = jnp.where(k < count, lax.rem(j, PARTS), PARTS)
        return carry

    lax.fori_loop(0, ROWS, index_row, 0)

    loads[4].wait()

    def split_row(i, carry):
        whole = inv[i]
        high = whole.astype(BF16)
        inv_split[i, :, :TILE] = high
        inv_split[i, :, TILE:] = (whole - high.astype(F32)).astype(BF16)
        return carry

    lax.fori_loop(0, ROWS, split_row, 0)

    def band_term(band, tiles, part, i):
        panel = panels[band][part]
        pieces = [
            panel[place[band, i * SLOTS + k]] * masks[pick[band, i * SLOTS + k]]
            for k in range(SLOTS)
        ]
        left = jnp.concatenate(pieces, axis=1)
        right = tiles[i].reshape(SLOTS * TILE, TILE)
        return jnp.dot(left, right, preferred_element_type=F32)

    def solve(resid, i):
        high = resid.astype(BF16).astype(F32)
        both = jnp.concatenate([high, resid - high], axis=0).astype(BF16)
        four = jnp.dot(both, inv_split[i], preferred_element_type=F32)
        two = four[:, :TILE] + four[:, TILE:]
        return two[:WIDTH] + two[WIDTH:]

    STEP = 4

    def finish(part, resid_of):
        def rows(n, carry):
            done = []
            for m in range(STEP):
                i = n * STEP + m
                result = solve(resid_of(i), i)
                results[part][i] = result
                done.append(result)
            for m in range(STEP // PARTS):
                tile = jnp.concatenate(done[m * PARTS : (m + 1) * PARTS], axis=0)
                outgoing[part][n * (STEP // PARTS) + m] = tile.astype(BF16)
            return carry

        lax.fori_loop(0, ROWS // STEP, rows, 0)

        @pl.when(level < LEVELS - 1)
        def _():
            spread(outgoing[part], DOWN, part, upper, (2, 1, 3, 0))

        store(part).start()

    def store(part):
        return pltpu.make_async_copy(
            results[part],
            out_hbm.at[0, :, pl.ds(part * WIDTH, WIDTH), :],
            out_sem.at[part],
        )

    def base_rows(part):
        def rows(n, carry):
            for m in range(STEP):
                i = n * STEP + m
                total = band_term(OWN, level_t, part, i) + band_term(ABOVE, up, part, i)
                rhs = rhs_vmem[i, part * WIDTH : (part + 1) * WIDTH, :]
                bases[part][i] = rhs - fold(total)
            return carry

        lax.fori_loop(0, ROWS // STEP, rows, 0)

    relay(OWN, 0)
    relay(ABOVE, 0)
    for n in (1, 2, 3):
        loads[n].wait()
    for part in range(PARTS):
        if part + 1 < PARTS:
            relay(OWN, part + 1)
            relay(ABOVE, part + 1)
        share(OWN, part)
        share(ABOVE, part)
        complete(OWN, part)
        complete(ABOVE, part)
        base_rows(part)

        @pl.when(level == 0)
        def _():
            finish(part, lambda i: bases[part][i])

    loads[5].wait()

    @pl.when(level > 0)
    def _():
        relay(DOWN, 0)
        for part in range(PARTS):
            if part + 1 < PARTS:
                relay(DOWN, part + 1)
            share(DOWN, part)
            complete(DOWN, part)
            finish(part, lambda i: bases[part][i] - fold(band_term(DOWN, down, part, i)))

    for part in range(PARTS):
        drain(OWN, part, 3)
        drain(ABOVE, part, 4)
        drain_rest(OWN, part)
        drain_rest(ABOVE, part)

        @pl.when(level < LEVELS - 1)
        def _():
            drain(DOWN, part, 4)

        @pl.when(level > 0)
        def _():
            drain_rest(DOWN, part)

        store(part).wait()


def shards(x_old, rhs, down_tiles, level_tiles, up_tiles, inverses, tile_cols, tile_counts):
    in_hbm = pl.BlockSpec(memory_space=pltpu.HBM)
    in_smem = pl.BlockSpec(memory_space=pltpu.SMEM)
    panel = pltpu.VMEM((32 * SHARD, ROWS, TILE), BF16)
    part = pltpu.VMEM((ROWS, WIDTH, TILE), F32)
    return pl.pallas_call(
        sweep,
        out_shape=jax.ShapeDtypeStruct(rhs.shape, F32),
        in_specs=[in_hbm] * 6 + [in_smem] * 2,
        out_specs=in_hbm,
        scratch_shapes=[panel] * (3 * PARTS)
        + [pltpu.VMEM((SHARD, ROWS, TILE), BF16)] * PARTS
        + [part] * (2 * PARTS)
        + [
            pltpu.VMEM((ROWS, ROWS, TILE), BF16),
            pltpu.VMEM((ROWS, ROWS, TILE), F32),
            pltpu.VMEM((ROWS, SLOTS, TILE, TILE), BF16),
            pltpu.VMEM((ROWS, SLOTS, TILE, TILE), BF16),
            pltpu.VMEM((ROWS, SLOTS, TILE, TILE), BF16),
            pltpu.VMEM((ROWS, TILE, TILE), F32),
            pltpu.VMEM((ROWS, TILE, 2 * TILE), BF16),
            pltpu.VMEM((PARTS + 1, ROWS, TILE), BF16),
            pltpu.SMEM((3, ROWS * SLOTS), jnp.int32),
            pltpu.SMEM((3, ROWS * SLOTS), jnp.int32),
            pltpu.SemaphoreType.DMA((6,)),
            pltpu.SemaphoreType.DMA((PARTS,)),
            pltpu.SemaphoreType.DMA((3 * PARTS * 3,)),
            pltpu.SemaphoreType.DMA((3 * PARTS * 5,)),
        ],
        compiler_params=pltpu.CompilerParams(
            collective_id=0, has_side_effects=True, vmem_limit_bytes=60 * 1024 * 1024
        ),
        name="sweep",
    )(x_old, rhs, down_tiles, level_tiles, up_tiles, inverses, tile_cols, tile_counts)


def solution(mesh):
    return jax.shard_map(
        shards,
        mesh=mesh,
        in_specs=(
            P("level", "grp", None, None),
            P("level", "grp", None, None),
            P("level", "grp", None, None, None),
            P("level", "grp", None, None, None),
            P("level", "grp", None, None, None),
            P("level", "grp", None, None),
            P("level", "grp", None, None),
            P("level", "grp", None),
        ),
        out_specs=P("level", "grp", None, None),
        check_vma=False,
    )
```

time: 426 us -> 80 us (0.19)
  waiting for transfers between devices: 365 us -> 0 us
  Pallas kernels: 0 us -> 75.4 us
  matrix products: 16.3 us -> 0 us
  between operations: 13.2 us -> 0.01 us
  local copies, waits for them, and re-layouts: 17.2 us -> 4.32 us
  starting transfers between devices: 7.73 us -> 0 us
  other arithmetic: 5.17 us -> 0 us
    all_gather x4 -> x0, waiting for transfers between devices: 190 us -> none  [the longest x3 141 us: level_turn(): gathered = lax.all_gather(outgoing, 'grp', axis=0, tiled=True)]
    ppermute x4 -> x0, waiting for transfers between devices: 174 us -> none  [from_behind(): return lax.ppermute(value, axis, pairs)]
    pallas_call x0 -> x1, Pallas kernels: none -> 75.4 us  [shards(): pl.pallas_call(sweep, out_shape=jax.ShapeDtypeStruct(rhs.shape, F32), in_...]
    dot_general x9 -> x0, matrix products: 16.3 us -> none  [the longest x5 12.3 us: band_term(): jnp.einsum('bkrc,bkcq->brq', pieces, tiles, preferred_element_type=jnp.fl...]
    gather x5 -> x0, local copies, waits for them, and re-layouts: 11.3 us -> none  [band_term(): pieces = source[cols]]
    ppermute x4 -> x0, starting transfers between devices: 7.64 us -> none  [from_behind(): return lax.ppermute(value, axis, pairs)]
  transfers between devices with their start and end apart: 8 -> 0, of which waited for: 8 -> 0; matrix products, arithmetic and copies ran while one was open for 3% -> 0% of each run, Pallas kernels for 0% -> 0%
where the time goes in v1:
time: 80 us; the launch traced here: 79.7 us
  Pallas kernels  75.4 us (94%)
  local copies, waits for them, and re-layouts  4.32 us (5%)
    pallas_call x1, Pallas kernels, shards(): pl.pallas_call(sweep, out_shape=jax.ShapeDtypeStruct(rhs.shape, F32), in_...  75.4 us
    unnamed x3, local copies, waits for them, and re-layouts  4.32 us

profile of v1, /device:TPU:7, one launch (start us, length us, event | category | flops | bytes accessed | tf_op | source)
XLA Modules:
  0.0 79.7 jit_solution(17352739087255105479)
XLA Ops:
  0.0 1.4 %copy.10.counts = s32[1,16,3]{2,1,0:T(8,128)} copy(s32[1,16,3]{1,0,2:T(1,128)} %param.15) | data formatting | bytes 384 | tf_op args[7]
  1.4 1.4 %copy.9.cols = s32[1,16,3,6]{3,2,1,0:T(4,128)} copy(s32[1,16,3,6]{1,0,3,2:T(1,128)} %param.14) | data formatting | bytes 2304 | tf_op args[6]
  2.8 75.4 %sweep.1 = f32[1,16,16,128]{3,2,1,0:T(8,128)} custom-call(bf16[1,16,16,128]{3,2,1,0:T(8,128)(2,1)} %x_hbm.1, f32[1,16,16,128]{3,2,1,0:T(8,128)} %rhs_hbm.1, bf16[1,16,6,128,128]{4,3,2,1,0:T(8,128)(2,1)} %down_hbm.1, bf16[1,16,6,128,128]{4,3,2,1,0:T(8,128)(2,1)} %level_hbm.1, bf16[1,16,6,128,128]{4,3,2,1,0:T(8,128)(2,1)} %up_hbm.1, ...), custom_call_target="tpu_custom_call" | custom-call | tf_op jit(solution)/shard_map/sweep/pallas_call | solution.py:318
  78.1 1.6 %copy.12 = f32[1,16,16,128]{3,2,1,0:T(8,128)} copy(f32[1,16,16,128]{3,2,1,0:T(8,128)} %sweep.1) | data formatting | bytes 262144

commit v2 on v1

v2 whole, which is shorter than its diff:
```python
import jax
import jax.numpy as jnp
from jax import lax
from jax.experimental import pallas as pl
from jax.experimental.pallas import tpu as pltpu
from jax.sharding import PartitionSpec as P

MESH = pl.DeviceIdType.MESH
ROWS = 16
SLOTS = 6
TILE = 128
LEVELS = 4
PARTS = 4
WIDTH = ROWS // PARTS
SHARD = ROWS // PARTS
GROUP = 4 * SHARD
HALF = 16 * SHARD
TURNS = 2
SUBS = PARTS // TURNS
STEP = 16
OWN, ABOVE, DOWN = 1, 2, 0
F32, BF16 = jnp.float32, jnp.bfloat16


def fold(total):
    while total.shape[0] > WIDTH:
        half = total.shape[0] // 2
        total = total[:half] + total[half:]
    return total


def sweep(
    x_hbm, rhs_hbm, down_hbm, level_hbm, up_hbm, inv_hbm, cols, counts, out_hbm,
    panel_down, panel_own, panel_above, work, work_above, outgoing, results, bases, resid,
    x_vmem, rhs_vmem, down, level_t, up, inv, inv_split, masks, place, pick,
    load_sem, out_sem, send_sem, recv_sem,
):
    panels = {DOWN: panel_down, OWN: panel_own, ABOVE: panel_above}
    level = lax.axis_index("level")
    grp = lax.axis_index("grp")
    core = lax.rem(grp, 2)
    y = lax.rem(lax.div(grp, 2), 4)
    z = lax.div(grp, 8)
    first = core == 0
    a = jnp.where(first, y, z)
    b = jnp.where(first, z, y)
    lower = lax.rem(level + LEVELS - 1, LEVELS)
    upper = lax.rem(level + 1, LEVELS)

    def device(at_level, at_a, at_b):
        at_y = jnp.where(first, at_a, at_b)
        at_z = jnp.where(first, at_b, at_a)
        return (at_level, at_z * 8 + at_y * 2 + core)

    sibling = (level, z * 8 + y * 2 + 1 - core)

    def turn(value, by):
        return lax.rem(value + by, 4)

    loads = [
        (x_hbm.at[0], x_vmem),
        (level_hbm.at[0], level_t),
        (up_hbm.at[0], up),
        (rhs_hbm.at[0, :, pl.ds(0, 8), :], rhs_vmem.at[0]),
        (rhs_hbm.at[0, :, pl.ds(8, 8), :], rhs_vmem.at[1]),
        (inv_hbm.at[0], inv),
        (down_hbm.at[0], down),
    ]
    loads = [pltpu.make_async_copy(src, dst, load_sem.at[n]) for n, (src, dst) in enumerate(loads)]
    for load in loads:
        load.start()

    barrier = pltpu.get_barrier_semaphore()
    partners = [sibling]
    partners += [device(level, turn(a, d), b) for d in (1, 2, 3)]
    partners += [device(level, a, turn(b, d)) for d in (1, 2, 3)]
    partners += [device(lower, turn(a, d), b) for d in (0, 1, 2, 3)]
    partners += [device(upper, turn(a, d), b) for d in (0, 1, 2, 3)]
    for partner in partners:
        pl.semaphore_signal(barrier, inc=1, device_id=partner, device_id_type=MESH)

    shard_at = (core * 16 + b * 4 + a) * SHARD
    shard = pl.ds(shard_at, SHARD)

    def group(at_core, at_b):
        return pl.ds((at_core * 16 + at_b * 4) * SHARD, GROUP)

    def half(at_core):
        return pl.ds(at_core * HALF, HALF)

    def recv(panel, part, which):
        return recv_sem.at[(panel * PARTS + part) * 5 + which]

    def sent(panel, part, which):
        return send_sem.at[(panel * PARTS + part) * 3 + which]

    def spread(source, panel, part, target, turns):
        for d in turns:
            pltpu.make_async_remote_copy(
                src_ref=source,
                dst_ref=panels[panel].at[part].at[shard],
                send_sem=sent(panel, part, 0),
                recv_sem=recv(panel, part, 0),
                device_id=device(target, turn(a, d), b),
                device_id_type=MESH,
            ).start()

    def wait_bytes(ref, sem):
        pltpu.make_async_copy(ref, ref, sem).wait()

    def to_sibling(panel, part, which):
        ref = panels[panel].at[part].at[which]
        pltpu.make_async_remote_copy(
            src_ref=ref,
            dst_ref=ref,
            send_sem=sent(panel, part, 2),
            recv_sem=recv(panel, part, 4),
            device_id=sibling,
            device_id_type=MESH,
        ).start()

    def relay(panel, part):
        ref = panels[panel].at[part]
        mine = ref.at[group(core, b)]
        if panel == OWN:
            wait_bytes(ref.at[pl.ds(0, 3 * SHARD)], recv(panel, part, 0))
        else:
            wait_bytes(mine, recv(panel, part, 0))
        for d in (2, 1, 3):
            pltpu.make_async_remote_copy(
                src_ref=mine,
                dst_ref=mine,
                send_sem=sent(panel, part, 1),
                recv_sem=recv(panel, part, d),
                device_id=device(level, a, turn(b, d)),
                device_id_type=MESH,
            ).start()
        to_sibling(panel, part, group(core, b))

    def share(panel, part):
        for d in (1, 3, 2):
            theirs = group(core, turn(b, 4 - d))
            wait_bytes(panels[panel].at[part].at[theirs], recv(panel, part, d))
            to_sibling(panel, part, theirs)

    def complete(panel, part):
        wait_bytes(panels[panel].at[part].at[half(1 - core)], recv(panel, part, 4))

    def drain(panel, part, shards):
        ref = panels[panel].at[part]
        wait_bytes(ref.at[pl.ds(0, shards * SHARD)], sent(panel, part, 0))

    def drain_rest(panel, part):
        ref = panels[panel].at[part]
        wait_bytes(ref.at[pl.ds(0, 3 * GROUP)], sent(panel, part, 1))
        wait_bytes(ref.at[pl.ds(0, 4 * GROUP)], sent(panel, part, 2))

    loads[0].wait()
    for part in range(PARTS):
        for j in range(SHARD):
            rows = [
                x_vmem[PARTS * j + q].astype(F32)[part * WIDTH : (part + 1) * WIDTH]
                for q in range(PARTS)
            ]
            panels[OWN][part, shard_at + j] = jnp.concatenate(rows, axis=0).astype(BF16)

    pl.semaphore_wait(barrier, len(partners))
    for part in range(PARTS):
        mine = panels[OWN].at[part, shard]
        spread(mine, OWN, part, level, (2, 1, 3))
        spread(mine, ABOVE, part, lower, (2, 1, 3, 0))

    row_group = lax.broadcasted_iota(jnp.int32, (ROWS, TILE), 0) // WIDTH
    for q in range(PARTS + 1):
        masks[q] = jnp.where(row_group == q, 1.0, 0.0).astype(BF16)

    def index_row(i, carry):
        for band in range(3):
            count = counts[band, 0, i]
            if band == ABOVE:
                count = jnp.where(level == LEVELS - 1, 0, count)
            for k in range(SLOTS):
                col = cols[band, k, 0, i]
                owner, j = lax.shift_right_logical(col, 4), lax.bitwise_and(col, 15)
                oz = lax.shift_right_logical(owner, 3)
                oy = lax.bitwise_and(lax.shift_right_logical(owner, 1), 3)
                even = lax.bitwise_and(owner, 1) == 0
                pos = jnp.where(even, oz * 4 + oy, 16 + oy * 4 + oz)
                place[band, i * SLOTS + k] = pos * SHARD + j // PARTS
                pick[band, i * SLOTS + k] = jnp.where(k < count, lax.rem(j, PARTS), PARTS)
        return carry

    lax.fori_loop(0, ROWS, index_row, 0)

    loads[5].wait()

    def split_row(i, carry):
        whole = inv[i]
        high = whole.astype(BF16)
        inv_split[i, :, :TILE] = high
        inv_split[i, :, TILE:] = (whole - high.astype(F32)).astype(BF16)
        return carry

    lax.fori_loop(0, ROWS, split_row, 0)

    def band_term(band, tiles, blocks, i):
        pieces = [
            blocks[place[band, i * SLOTS + k]] * masks[pick[band, i * SLOTS + k]]
            for k in range(SLOTS)
        ]
        left = jnp.concatenate(pieces, axis=1)
        right = tiles[i].reshape(SLOTS * TILE, TILE)
        return jnp.dot(left, right, preferred_element_type=F32)

    def solve(rest, i):
        high = rest.astype(BF16).astype(F32)
        both = jnp.concatenate([high, rest - high], axis=0).astype(BF16)
        four = jnp.dot(both, inv_split[i], preferred_element_type=F32)
        two = four[:, :TILE] + four[:, TILE:]
        return two[:WIDTH] + two[WIDTH:]

    def all_rows(step):
        if STEP == ROWS:
            step(0)
        else:
            lax.fori_loop(0, ROWS // STEP, lambda n, carry: (step(n), carry)[1], 0)

    def base_rows(turn_, sub, part):
        def step(n):
            for m in range(STEP):
                i = n * STEP + m
                total = band_term(OWN, level_t, work, i) + band_term(ABOVE, up, work_above, i)
                rhs = rhs_vmem[turn_, i, sub * WIDTH : (sub + 1) * WIDTH, :]
                bases[part, i] = rhs - fold(total)

        all_rows(step)

    def down_rows(part):
        def step(n):
            for m in range(STEP):
                i = n * STEP + m
                resid[i] = bases[part, i] - fold(band_term(DOWN, down, work, i))

        all_rows(step)

    def finish(turn_, sub, part, rest_of):
        def step(n):
            done = []
            for m in range(STEP):
                i = n * STEP + m
                result = solve(rest_of(i), i)
                results[turn_, i, sub * WIDTH : (sub + 1) * WIDTH, :] = result
                done.append(result)
            for m in range(STEP // PARTS):
                tile = jnp.concatenate(done[m * PARTS : (m + 1) * PARTS], axis=0)
                outgoing[part, n * (STEP // PARTS) + m] = tile.astype(BF16)

        all_rows(step)

        @pl.when(level < LEVELS - 1)
        def _():
            spread(outgoing.at[part], DOWN, part, upper, (2, 1, 3, 0))

    def store(turn_):
        return pltpu.make_async_copy(
            results.at[turn_], out_hbm.at[0, :, pl.ds(turn_ * 8, 8), :], out_sem.at[turn_]
        )

    relay(OWN, 0)
    relay(ABOVE, 0)
    for n in (1, 2, 3, 4):
        loads[n].wait()

    def base_turn(turn_, carry):
        for sub in range(SUBS):
            part = turn_ * SUBS + sub

            @pl.when(part + 1 < PARTS)
            def _():
                relay(OWN, part + 1)
                relay(ABOVE, part + 1)

            share(OWN, part)
            share(ABOVE, part)
            complete(OWN, part)
            work[...] = panel_own[part]
            complete(ABOVE, part)
            work_above[...] = panel_above[part]
            base_rows(turn_, sub, part)

            @pl.when(level == 0)
            def _():
                finish(turn_, sub, part, lambda i: bases[part, i])

        @pl.when(level == 0)
        def _():
            store(turn_).start()

        return carry

    lax.fori_loop(0, TURNS, base_turn, 0)
    loads[6].wait()

    @pl.when(level > 0)
    def _():
        relay(DOWN, 0)

        def down_turn(turn_, carry):
            for sub in range(SUBS):
                part = turn_ * SUBS + sub

                @pl.when(part + 1 < PARTS)
                def _():
                    relay(DOWN, part + 1)

                share(DOWN, part)
                complete(DOWN, part)
                work[...] = panel_down[part]
                down_rows(part)
                finish(turn_, sub, part, lambda i: resid[i])

            store(turn_).start()
            return carry

        lax.fori_loop(0, TURNS, down_turn, 0)

    for turn_ in range(TURNS):
        store(turn_).wait()
    for part in range(PARTS):
        drain(OWN, part, 3)
        drain(ABOVE, part, 4)
        drain_rest(OWN, part)
        drain_rest(ABOVE, part)

        @pl.when(level < LEVELS - 1)
        def _():
            drain(DOWN, part, 4)

        @pl.when(level > 0)
        def _():
            drain_rest(DOWN, part)


def shards(x_old, rhs, down_tiles, level_tiles, up_tiles, inverses, tile_cols, tile_counts):
    cols = tile_cols.transpose(2, 3, 0, 1)
    counts = tile_counts.transpose(2, 0, 1)
    in_hbm = pl.BlockSpec(memory_space=pltpu.HBM)
    in_smem = pl.BlockSpec(memory_space=pltpu.SMEM)
    panel = pltpu.VMEM((PARTS, 32 * SHARD, ROWS, TILE), BF16)
    return pl.pallas_call(
        sweep,
        out_shape=jax.ShapeDtypeStruct(rhs.shape, F32),
        in_specs=[in_hbm] * 6 + [in_smem] * 2,
        out_specs=in_hbm,
        scratch_shapes=[panel] * 3
        + [
            pltpu.VMEM((32 * SHARD, ROWS, TILE), BF16),
            pltpu.VMEM((32 * SHARD, ROWS, TILE), BF16),
            pltpu.VMEM((PARTS, SHARD, ROWS, TILE), BF16),
            pltpu.VMEM((TURNS, ROWS, 8, TILE), F32),
            pltpu.VMEM((PARTS, ROWS, WIDTH, TILE), F32),
            pltpu.VMEM((ROWS, WIDTH, TILE), F32),
            pltpu.VMEM((ROWS, ROWS, TILE), BF16),
            pltpu.VMEM((TURNS, ROWS, 8, TILE), F32),
            pltpu.VMEM((ROWS, SLOTS, TILE, TILE), BF16),
            pltpu.VMEM((ROWS, SLOTS, TILE, TILE), BF16),
            pltpu.VMEM((ROWS, SLOTS, TILE, TILE), BF16),
            pltpu.VMEM((ROWS, TILE, TILE), F32),
            pltpu.VMEM((ROWS, TILE, 2 * TILE), BF16),
            pltpu.VMEM((PARTS + 1, ROWS, TILE), BF16),
            pltpu.SMEM((3, ROWS * SLOTS), jnp.int32),
            pltpu.SMEM((3, ROWS * SLOTS), jnp.int32),
            pltpu.SemaphoreType.DMA((7,)),
            pltpu.SemaphoreType.DMA((TURNS,)),
            pltpu.SemaphoreType.DMA((3 * PARTS * 3,)),
            pltpu.SemaphoreType.DMA((3 * PARTS * 5,)),
        ],
        compiler_params=pltpu.CompilerParams(
            collective_id=0, has_side_effects=True, vmem_limit_bytes=60 * 1024 * 1024
        ),
        name="sweep",
    )(x_old, rhs, down_tiles, level_tiles, up_tiles, inverses, cols, counts)


def solution(mesh):
    return jax.shard_map(
        shards,
        mesh=mesh,
        in_specs=(
            P("level", "grp", None, None),
            P("level", "grp", None, None),
            P("level", "grp", None, None, None),
            P("level", "grp", None, None, None),
            P("level", "grp", None, None, None),
            P("level", "grp", None, None),
            P("level", "grp", None, None),
            P("level", "grp", None),
        ),
        out_specs=P("level", "grp", None, None),
        check_vma=False,
    )
```

time: 80 us -> 69.1 us (0.86)
  Pallas kernels: 75.4 us -> 67.3 us
  local copies, waits for them, and re-layouts: 4.32 us -> 1.57 us
    pallas_call x1, Pallas kernels: 75.4 us -> 67.3 us  [shards(): pl.pallas_call(sweep, out_shape=jax.ShapeDtypeStruct(rhs.shape, F32), in_...]
    unnamed x3 -> x1, local copies, waits for them, and re-layouts: 4.32 us -> 1.57 us
where the time goes in v2:
time: 69.1 us; the launch traced here: 68.9 us
  Pallas kernels  67.3 us (97%)
  local copies, waits for them, and re-layouts  1.57 us (2%)
    pallas_call x1, Pallas kernels, shards(): pl.pallas_call(sweep, out_shape=jax.ShapeDtypeStruct(rhs.shape, F32), in_...  67.3 us
    unnamed x1, local copies, waits for them, and re-layouts  1.57 us

profile of v2, /device:TPU:7, one launch (start us, length us, event | category | flops | bytes accessed | tf_op | source)
XLA Modules:
  0.0 68.9 jit_solution(16045661386684475119)
XLA Ops:
  0.0 67.3 %sweep.1 = f32[1,16,16,128]{3,2,1,0:T(8,128)} custom-call(bf16[1,16,16,128]{3,2,1,0:T(8,128)(2,1)} %x_hbm.1, f32[1,16,16,128]{3,2,1,0:T(8,128)} %rhs_hbm.1, bf16[1,16,6,128,128]{4,3,2,1,0:T(8,128)(2,1)} %down_hbm.1, bf16[1,16,6,128,128]{4,3,2,1,0:T(8,128)(2,1)} %level_hbm.1, bf16[1,16,6,128,128]{4,3,2,1,0:T(8,128)(2,1)} %up_hbm.1, ...), custom_call_target="tpu_custom_call" | custom-call | tf_op jit(solution)/shard_map/sweep/pallas_call | solution.py:350
  67.3 1.6 %copy.10 = f32[1,16,16,128]{3,2,1,0:T(8,128)} copy(f32[1,16,16,128]{3,2,1,0:T(8,128)} %sweep.1) | data formatting | bytes 262144

commit v3 on v2

--- a/solution.py
+++ b/solution.py
@@ -19,6 +19,7 @@
 SUBS = PARTS // TURNS
 STEP = 16
 OWN, ABOVE, DOWN = 1, 2, 0
+AHEAD = 2
 F32, BF16 = jnp.float32, jnp.bfloat16
 
 
@@ -41,21 +42,24 @@
     core = lax.rem(grp, 2)
     y = lax.rem(lax.div(grp, 2), 4)
     z = lax.div(grp, 8)
-    first = core == 0
-    a = jnp.where(first, y, z)
-    b = jnp.where(first, z, y)
+    def turn(value, by):
+        return lax.rem(value + by, 4)
+
     lower = lax.rem(level + LEVELS - 1, LEVELS)
     upper = lax.rem(level + 1, LEVELS)
-
-    def device(at_level, at_a, at_b):
-        at_y = jnp.where(first, at_a, at_b)
-        at_z = jnp.where(first, at_b, at_a)
+    along_y = {OWN: core == 0, ABOVE: core == 1, DOWN: core == 1}
+    place_a = {panel: jnp.where(first, y, z) for panel, first in along_y.items()}
+    place_b = {panel: jnp.where(first, z, y) for panel, first in along_y.items()}
+
+    def device(panel, at_level, at_a, at_b):
+        at_y = jnp.where(along_y[panel], at_a, at_b)
+        at_z = jnp.where(along_y[panel], at_b, at_a)
         return (at_level, at_z * 8 + at_y * 2 + core)
 
+    def around(panel, at_level, by_a, by_b):
+        return device(panel, at_level, turn(place_a[panel], by_a), turn(place_b[panel], by_b))
+
     sibling = (level, z * 8 + y * 2 + 1 - core)
-
-    def turn(value, by):
-        return lax.rem(value + by, 4)
 
     loads = [
         (x_hbm.at[0], x_vmem),
@@ -72,36 +76,39 @@
 
     barrier = pltpu.get_barrier_semaphore()
     partners = [sibling]
-    partners += [device(level, turn(a, d), b) for d in (1, 2, 3)]
-    partners += [device(level, a, turn(b, d)) for d in (1, 2, 3)]
-    partners += [device(lower, turn(a, d), b) for d in (0, 1, 2, 3)]
-    partners += [device(upper, turn(a, d), b) for d in (0, 1, 2, 3)]
+    partners += [around(OWN, level, d, 0) for d in (1, 2, 3)]
+    partners += [around(OWN, level, 0, d) for d in (1, 2, 3)]
+    partners += [around(ABOVE, lower, d, 0) for d in (0, 1, 2, 3)]
+    partners += [around(DOWN, upper, d, 0) for d in (0, 1, 2, 3)]
     for partner in partners:
         pl.semaphore_signal(barrier, inc=1, device_id=partner, device_id_type=MESH)
 
-    shard_at = (core * 16 + b * 4 + a) * SHARD
-    shard = pl.ds(shard_at, SHARD)
-
-    def group(at_core, at_b):
-        return pl.ds((at_core * 16 + at_b * 4) * SHARD, GROUP)
+    def shard_at(panel, by_a):
+        return (core * 16 + place_b[panel] * 4 + turn(place_a[panel], by_a)) * SHARD
+
+    def shard(panel, by_a=0):
+        return pl.ds(shard_at(panel, by_a), SHARD)
+
+    def group(panel, by_b):
+        return pl.ds((core * 16 + turn(place_b[panel], by_b) * 4) * SHARD, GROUP)
 
     def half(at_core):
         return pl.ds(at_core * HALF, HALF)
 
     def recv(panel, part, which):
-        return recv_sem.at[(panel * PARTS + part) * 5 + which]
+        return recv_sem.at[(panel * PARTS + part) * 8 + which]
 
     def sent(panel, part, which):
-        return send_sem.at[(panel * PARTS + part) * 3 + which]
+        return send_sem.at[(panel * PARTS + part) * 4 + which]
 
     def spread(source, panel, part, target, turns):
         for d in turns:
             pltpu.make_async_remote_copy(
                 src_ref=source,
-                dst_ref=panels[panel].at[part].at[shard],
+                dst_ref=panels[panel].at[part, shard(panel)],
                 send_sem=sent(panel, part, 0),
-                recv_sem=recv(panel, part, 0),
-                device_id=device(target, turn(a, d), b),
+                recv_sem=recv(panel, part, d),
+                device_id=around(panel, target, d, 0),
                 device_id_type=MESH,
             ).start()
 
@@ -119,28 +126,28 @@
             device_id_type=MESH,
         ).start()
 
-    def relay(panel, part):
-        ref = panels[panel].at[part]
-        mine = ref.at[group(core, b)]
-        if panel == OWN:
-            wait_bytes(ref.at[pl.ds(0, 3 * SHARD)], recv(panel, part, 0))
-        else:
-            wait_bytes(mine, recv(panel, part, 0))
+    def send_on(panel, part, by_a):
+        ref = panels[panel].at[part, shard(panel, by_a)]
         for d in (2, 1, 3):
             pltpu.make_async_remote_copy(
-                src_ref=mine,
-                dst_ref=mine,
+                src_ref=ref,
+                dst_ref=ref,
                 send_sem=sent(panel, part, 1),
-                recv_sem=recv(panel, part, d),
-                device_id=device(level, a, turn(b, d)),
+                recv_sem=recv(panel, part, 4 + d),
+                device_id=around(panel, level, 0, d),
                 device_id_type=MESH,
             ).start()
-        to_sibling(panel, part, group(core, b))
+
+    def relay(panel, part):
+        for d in (1, 3, 2) if panel == OWN else (0, 1, 3, 2):
+            wait_bytes(panels[panel].at[part, shard(panel, 4 - d)], recv(panel, part, d))
+            send_on(panel, part, 4 - d)
+        to_sibling(panel, part, group(panel, 0))
 
     def share(panel, part):
         for d in (1, 3, 2):
-            theirs = group(core, turn(b, 4 - d))
-            wait_bytes(panels[panel].at[part].at[theirs], recv(panel, part, d))
+            theirs = group(panel, 4 - d)
+            wait_bytes(panels[panel].at[part, theirs], recv(panel, part, 4 + d))
             to_sibling(panel, part, theirs)
 
     def complete(panel, part):
@@ -162,13 +169,18 @@
                 x_vmem[PARTS * j + q].astype(F32)[part * WIDTH : (part + 1) * WIDTH]
                 for q in range(PARTS)
             ]
-            panels[OWN][part, shard_at + j] = jnp.concatenate(rows, axis=0).astype(BF16)
+            panels[OWN][part, shard_at(OWN, 0) + j] = jnp.concatenate(rows, axis=0).astype(BF16)
 
     pl.semaphore_wait(barrier, len(partners))
     for part in range(PARTS):
-        mine = panels[OWN].at[part, shard]
+        mine = panels[OWN].at[part, shard(OWN)]
         spread(mine, OWN, part, level, (2, 1, 3))
-        spread(mine, ABOVE, part, lower, (2, 1, 3, 0))
+
+        @pl.when(level > 0)
+        def _():
+            spread(mine, ABOVE, part, lower, (2, 1, 3, 0))
+
+        send_on(OWN, part, 0)
 
     row_group = lax.broadcasted_iota(jnp.int32, (ROWS, TILE), 0) // WIDTH
     for q in range(PARTS + 1):
@@ -185,7 +197,9 @@
                 oz = lax.shift_right_logical(owner, 3)
                 oy = lax.bitwise_and(lax.shift_right_logical(owner, 1), 3)
                 even = lax.bitwise_and(owner, 1) == 0
-                pos = jnp.where(even, oz * 4 + oy, 16 + oy * 4 + oz)
+                pos = jnp.where(even, 0, 16) + jnp.where(
+                    even == (band == OWN), oz * 4 + oy, oy * 4 + oz
+                )
                 place[band, i * SLOTS + k] = pos * SHARD + j // PARTS
                 pick[band, i * SLOTS + k] = jnp.where(k < count, lax.rem(j, PARTS), PARTS)
         return carry
@@ -266,8 +280,20 @@
             results.at[turn_], out_hbm.at[0, :, pl.ds(turn_ * 8, 8), :], out_sem.at[turn_]
         )
 
-    relay(OWN, 0)
-    relay(ABOVE, 0)
+    def relay_both(part):
+        relay(OWN, part)
+
+        @pl.when(level < LEVELS - 1)
+        def _():
+            relay(ABOVE, part)
+
+    for part in range(AHEAD):
+        relay_both(part)
+
+    @pl.when(level == LEVELS - 1)
+    def _():
+        work_above[...] = jnp.zeros_like(work_above)
+
     for n in (1, 2, 3, 4):
         loads[n].wait()
 
@@ -275,23 +301,34 @@
         for sub in range(SUBS):
             part = turn_ * SUBS + sub
 
-            @pl.when(part + 1 < PARTS)
+            @pl.when(part + AHEAD < PARTS)
             def _():
-                relay(OWN, part + 1)
-                relay(ABOVE, part + 1)
+                relay_both(part + AHEAD)
 
             share(OWN, part)
-            share(ABOVE, part)
+
+            @pl.when(level < LEVELS - 1)
+            def _():
+                share(ABOVE, part)
+
             complete(OWN, part)
             work[...] = panel_own[part]
-            complete(ABOVE, part)
-            work_above[...] = panel_above[part]
+
+            @pl.when(level < LEVELS - 1)
+            def _():
+                complete(ABOVE, part)
+                work_above[...] = panel_above[part]
+
             base_rows(turn_, sub, part)
 
             @pl.when(level == 0)
             def _():
                 finish(turn_, sub, part, lambda i: bases[part, i])
 
+            @pl.when((level == 1) & (part > 0))
+            def _():
+                relay(DOWN, part - 1)
+
         @pl.when(level == 0)
         def _():
             store(turn_).start()
@@ -303,13 +340,15 @@
 
     @pl.when(level > 0)
     def _():
-        relay(DOWN, 0)
+        @pl.when(level > 1)
+        def _():
+            relay(DOWN, 0)
 
         def down_turn(turn_, carry):
             for sub in range(SUBS):
                 part = turn_ * SUBS + sub
 
-                @pl.when(part + 1 < PARTS)
+                @pl.when((part + 1 < PARTS) & ((level > 1) | (part + 2 == PARTS)))
                 def _():
                     relay(DOWN, part + 1)
 
@@ -328,16 +367,16 @@
         store(turn_).wait()
     for part in range(PARTS):
         drain(OWN, part, 3)
-        drain(ABOVE, part, 4)
         drain_rest(OWN, part)
-        drain_rest(ABOVE, part)
 
         @pl.when(level < LEVELS - 1)
         def _():
             drain(DOWN, part, 4)
+            drain_rest(ABOVE, part)
 
         @pl.when(level > 0)
         def _():
+            drain(ABOVE, part, 4)
             drain_rest(DOWN, part)
 
 
@@ -372,8 +411,8 @@
             pltpu.SMEM((3, ROWS * SLOTS), jnp.int32),
             pltpu.SemaphoreType.DMA((7,)),
             pltpu.SemaphoreType.DMA((TURNS,)),
-            pltpu.SemaphoreType.DMA((3 * PARTS * 3,)),
-            pltpu.SemaphoreType.DMA((3 * PARTS * 5,)),
+            pltpu.SemaphoreType.DMA((3 * PARTS * 4,)),
+            pltpu.SemaphoreType.DMA((3 * PARTS * 8,)),
         ],
         compiler_params=pltpu.CompilerParams(
             collective_id=0, has_side_effects=True, vmem_limit_bytes=60 * 1024 * 1024

time: 69.1 us -> 64.3 us (0.931)
  Pallas kernels: 67.3 us -> 62.5 us
    pallas_call x1, Pallas kernels: 67.3 us -> 62.5 us  [shards(): pl.pallas_call(sweep, out_shape=jax.ShapeDtypeStruct(rhs.shape, F32), in_...]
where the time goes in v3:
time: 64.3 us; the launch traced here: 64.1 us
  Pallas kernels  62.5 us (97%)
  local copies, waits for them, and re-layouts  1.57 us (2%)
    pallas_call x1, Pallas kernels, shards(): pl.pallas_call(sweep, out_shape=jax.ShapeDtypeStruct(rhs.shape, F32), in_...  62.5 us
    unnamed x1, local copies, waits for them, and re-layouts  1.57 us

profile of v3, /device:TPU:7, one launch (start us, length us, event | category | flops | bytes accessed | tf_op | source)
XLA Modules:
  0.0 64.1 jit_solution(7358177720716790565)
XLA Ops:
  0.0 62.5 %sweep.1 = f32[1,16,16,128]{3,2,1,0:T(8,128)} custom-call(bf16[1,16,16,128]{3,2,1,0:T(8,128)(2,1)} %x_hbm.1, f32[1,16,16,128]{3,2,1,0:T(8,128)} %rhs_hbm.1, bf16[1,16,6,128,128]{4,3,2,1,0:T(8,128)(2,1)} %down_hbm.1, bf16[1,16,6,128,128]{4,3,2,1,0:T(8,128)(2,1)} %level_hbm.1, bf16[1,16,6,128,128]{4,3,2,1,0:T(8,128)(2,1)} %up_hbm.1, ...), custom_call_target="tpu_custom_call" | custom-call | tf_op jit(solution)/shard_map/sweep/pallas_call | solution.py:389
  62.5 1.6 %copy.10 = f32[1,16,16,128]{3,2,1,0:T(8,128)} copy(f32[1,16,16,128]{3,2,1,0:T(8,128)} %sweep.1) | data formatting | bytes 262144

commit v4 on v3

--- a/solution.py
+++ b/solution.py
@@ -20,6 +20,12 @@
 STEP = 16
 OWN, ABOVE, DOWN = 1, 2, 0
 AHEAD = 2
+DOWN_AHEAD = 2
+LATE_AHEAD = 2
+BETWEEN = 1
+S2_ORDER = (2, 1, 3)
+S1_ORDER = (2, 1, 3, 0)
+BASE_FROM = 2
 F32, BF16 = jnp.float32, jnp.bfloat16
 
 
@@ -31,10 +37,10 @@
 
 
 def sweep(
-    x_hbm, rhs_hbm, down_hbm, level_hbm, up_hbm, inv_hbm, cols, counts, out_hbm,
+    x_hbm, rhs_hbm, down_hbm, level_hbm, up_hbm, inv_hbm, cols, counts, out_ref,
     panel_down, panel_own, panel_above, work, work_above, outgoing, results, bases, resid,
     x_vmem, rhs_vmem, down, level_t, up, inv, inv_split, masks, place, pick,
-    load_sem, out_sem, send_sem, recv_sem,
+    load_sem, send_sem, recv_sem,
 ):
     panels = {DOWN: panel_down, OWN: panel_own, ABOVE: panel_above}
     level = lax.axis_index("level")
@@ -128,7 +134,7 @@
 
     def send_on(panel, part, by_a):
         ref = panels[panel].at[part, shard(panel, by_a)]
-        for d in (2, 1, 3):
+        for d in S2_ORDER:
             pltpu.make_async_remote_copy(
                 src_ref=ref,
                 dst_ref=ref,
@@ -273,12 +279,7 @@
 
         @pl.when(level < LEVELS - 1)
         def _():
-            spread(outgoing.at[part], DOWN, part, upper, (2, 1, 3, 0))
-
-    def store(turn_):
-        return pltpu.make_async_copy(
-            results.at[turn_], out_hbm.at[0, :, pl.ds(turn_ * 8, 8), :], out_sem.at[turn_]
-        )
+            spread(outgoing.at[part], DOWN, part, upper, S1_ORDER)
 
     def relay_both(part):
         relay(OWN, part)
@@ -286,6 +287,13 @@
         @pl.when(level < LEVELS - 1)
         def _():
             relay(ABOVE, part)
+
+    def share_both(part):
+        share(OWN, part)
+
+        @pl.when(level < LEVELS - 1)
+        def _():
+            share(ABOVE, part)
 
     for part in range(AHEAD):
         relay_both(part)
@@ -305,11 +313,13 @@
             def _():
                 relay_both(part + AHEAD)
 
-            share(OWN, part)
-
-            @pl.when(level < LEVELS - 1)
-            def _():
-                share(ABOVE, part)
+            @pl.when(part <= BASE_FROM)
+            def _():
+                share_both(part)
+
+            @pl.when((part >= BASE_FROM) & (part + 1 < PARTS))
+            def _():
+                share_both(part + 1)
 
             complete(OWN, part)
             work[...] = panel_own[part]
@@ -325,13 +335,9 @@
             def _():
                 finish(turn_, sub, part, lambda i: bases[part, i])
 
-            @pl.when((level == 1) & (part > 0))
-            def _():
-                relay(DOWN, part - 1)
-
-        @pl.when(level == 0)
-        def _():
-            store(turn_).start()
+            @pl.when((level == 1) & (part >= BETWEEN))
+            def _():
+                relay(DOWN, part - BETWEEN)
 
         return carry
 
@@ -342,15 +348,18 @@
     def _():
         @pl.when(level > 1)
         def _():
-            relay(DOWN, 0)
+            for part in range(LATE_AHEAD):
+                relay(DOWN, part)
 
         def down_turn(turn_, carry):
             for sub in range(SUBS):
                 part = turn_ * SUBS + sub
 
-                @pl.when((part + 1 < PARTS) & ((level > 1) | (part + 2 == PARTS)))
+                later = part + jnp.where(level > 1, LATE_AHEAD, DOWN_AHEAD)
+
+                @pl.when((later < PARTS) & ((level > 1) | (later >= PARTS - BETWEEN)))
                 def _():
-                    relay(DOWN, part + 1)
+                    relay(DOWN, later)
 
                 share(DOWN, part)
                 complete(DOWN, part)
@@ -358,13 +367,12 @@
                 down_rows(part)
                 finish(turn_, sub, part, lambda i: resid[i])
 
-            store(turn_).start()
             return carry
 
         lax.fori_loop(0, TURNS, down_turn, 0)
 
     for turn_ in range(TURNS):
-        store(turn_).wait()
+        out_ref[0, :, turn_ * 8 : (turn_ + 1) * 8, :] = results[turn_]
     for part in range(PARTS):
         drain(OWN, part, 3)
         drain_rest(OWN, part)
@@ -388,9 +396,9 @@
     panel = pltpu.VMEM((PARTS, 32 * SHARD, ROWS, TILE), BF16)
     return pl.pallas_call(
         sweep,
-        out_shape=jax.ShapeDtypeStruct(rhs.shape, F32),
+        out_shape=pltpu.VMEM(rhs.shape, F32),
         in_specs=[in_hbm] * 6 + [in_smem] * 2,
-        out_specs=in_hbm,
+        out_specs=pl.BlockSpec(memory_space=pltpu.VMEM),
         scratch_shapes=[panel] * 3
         + [
             pltpu.VMEM((32 * SHARD, ROWS, TILE), BF16),
@@ -410,7 +418,6 @@
             pltpu.SMEM((3, ROWS * SLOTS), jnp.int32),
             pltpu.SMEM((3, ROWS * SLOTS), jnp.int32),
             pltpu.SemaphoreType.DMA((7,)),
-            pltpu.SemaphoreType.DMA((TURNS,)),
             pltpu.SemaphoreType.DMA((3 * PARTS * 4,)),
             pltpu.SemaphoreType.DMA((3 * PARTS * 8,)),
         ],

time: 64.3 us -> 62 us (0.964)
  Pallas kernels: 62.5 us -> 61.2 us
  local copies, waits for them, and re-layouts: 1.57 us -> 0.66 us
    pallas_call x1, Pallas kernels: 62.5 us -> 61.2 us  [shards(): pl.pallas_call(sweep, out_shape=pltpu.VMEM(rhs.shape, F32), in_specs=[in_...]
    unnamed x1, local copies, waits for them, and re-layouts: 1.57 us -> 0.66 us
where the time goes in v4:
time: 62 us; the launch traced here: 61.8 us
  Pallas kernels  61.2 us (99%)
  local copies, waits for them, and re-layouts  0.66 us (1%)
    pallas_call x1, Pallas kernels, shards(): pl.pallas_call(sweep, out_shape=pltpu.VMEM(rhs.shape, F32), in_specs=[in_...  61.2 us

profile of v4, /device:TPU:7, one launch (start us, length us, event | category | flops | bytes accessed | tf_op | source)
XLA Modules:
  0.0 61.8 jit_solution(2508245027735036662)
XLA Ops:
  0.0 61.2 %sweep.1 = f32[1,16,16,128]{3,2,1,0:T(8,128)S(1)} custom-call(bf16[1,16,16,128]{3,2,1,0:T(8,128)(2,1)} %x_hbm.1, f32[1,16,16,128]{3,2,1,0:T(8,128)} %rhs_hbm.1, bf16[1,16,6,128,128]{4,3,2,1,0:T(8,128)(2,1)} %down_hbm.1, bf16[1,16,6,128,128]{4,3,2,1,0:T(8,128)(2,1)} %level_hbm.1, bf16[1,16,6,128,128]{4,3,2,1,0:T(8,128)(2,1)} %up_hbm.1, ...), custom_call_target="tpu_custom_call" | custom-call | tf_op jit(solution)/shard_map/sweep/pallas_call | solution.py:397
  61.2 0.7 %copy.10 = f32[1,16,16,128]{3,2,1,0:T(8,128)} copy(f32[1,16,16,128]{3,2,1,0:T(8,128)S(1)} %sweep.1) | data formatting | bytes 262144

commit v5 on v4

--- a/solution.py
+++ b/solution.py
@@ -19,13 +19,13 @@
 SUBS = PARTS // TURNS
 STEP = 16
 OWN, ABOVE, DOWN = 1, 2, 0
-AHEAD = 2
+AHEAD = 3
 DOWN_AHEAD = 2
 LATE_AHEAD = 2
 BETWEEN = 1
 S2_ORDER = (2, 1, 3)
 S1_ORDER = (2, 1, 3, 0)
-BASE_FROM = 2
+BASE_FROM = 1
 F32, BF16 = jnp.float32, jnp.bfloat16
 
 
@@ -167,26 +167,6 @@
         ref = panels[panel].at[part]
         wait_bytes(ref.at[pl.ds(0, 3 * GROUP)], sent(panel, part, 1))
         wait_bytes(ref.at[pl.ds(0, 4 * GROUP)], sent(panel, part, 2))
-
-    loads[0].wait()
-    for part in range(PARTS):
-        for j in range(SHARD):
-            rows = [
-                x_vmem[PARTS * j + q].astype(F32)[part * WIDTH : (part + 1) * WIDTH]
-                for q in range(PARTS)
-            ]
-            panels[OWN][part, shard_at(OWN, 0) + j] = jnp.concatenate(rows, axis=0).astype(BF16)
-
-    pl.semaphore_wait(barrier, len(partners))
-    for part in range(PARTS):
-        mine = panels[OWN].at[part, shard(OWN)]
-        spread(mine, OWN, part, level, (2, 1, 3))
-
-        @pl.when(level > 0)
-        def _():
-            spread(mine, ABOVE, part, lower, (2, 1, 3, 0))
-
-        send_on(OWN, part, 0)
 
     row_group = lax.broadcasted_iota(jnp.int32, (ROWS, TILE), 0) // WIDTH
     for q in range(PARTS + 1):
@@ -211,6 +191,26 @@
         return carry
 
     lax.fori_loop(0, ROWS, index_row, 0)
+
+    loads[0].wait()
+    for part in range(PARTS):
+        for j in range(SHARD):
+            rows = [
+                x_vmem[PARTS * j + q].astype(F32)[part * WIDTH : (part + 1) * WIDTH]
+                for q in range(PARTS)
+            ]
+            panels[OWN][part, shard_at(OWN, 0) + j] = jnp.concatenate(rows, axis=0).astype(BF16)
+
+    pl.semaphore_wait(barrier, len(partners))
+    for part in range(PARTS):
+        mine = panels[OWN].at[part, shard(OWN)]
+        spread(mine, OWN, part, level, (2, 1, 3))
+
+        @pl.when(level > 0)
+        def _():
+            spread(mine, ABOVE, part, lower, (2, 1, 3, 0))
+
+        send_on(OWN, part, 0)
 
     loads[5].wait()
 

time: 62 us -> 61.7 us (level)
  no operation moved by 1% of the time
where the time goes in v5:
time: 61.7 us; the launch traced here: 61.5 us
  Pallas kernels  60.8 us (99%)
  local copies, waits for them, and re-layouts  0.66 us (1%)
    pallas_call x1, Pallas kernels, shards(): pl.pallas_call(sweep, out_shape=pltpu.VMEM(rhs.shape, F32), in_specs=[in_...  60.8 us

profile of v5, /device:TPU:7, one launch (start us, length us, event | category | flops | bytes accessed | tf_op | source)
XLA Modules:
  0.0 61.5 jit_solution(1292710249716249232)
XLA Ops:
  0.0 60.8 %sweep.1 = f32[1,16,16,128]{3,2,1,0:T(8,128)S(1)} custom-call(bf16[1,16,16,128]{3,2,1,0:T(8,128)(2,1)} %x_hbm.1, f32[1,16,16,128]{3,2,1,0:T(8,128)} %rhs_hbm.1, bf16[1,16,6,128,128]{4,3,2,1,0:T(8,128)(2,1)} %down_hbm.1, bf16[1,16,6,128,128]{4,3,2,1,0:T(8,128)(2,1)} %level_hbm.1, bf16[1,16,6,128,128]{4,3,2,1,0:T(8,128)(2,1)} %up_hbm.1, ...), custom_call_target="tpu_custom_call" | custom-call | tf_op jit(solution)/shard_map/sweep/pallas_call | solution.py:397
  60.9 0.7 %copy.10 = f32[1,16,16,128]{3,2,1,0:T(8,128)} copy(f32[1,16,16,128]{3,2,1,0:T(8,128)S(1)} %sweep.1) | data formatting | bytes 262144

commit v6 on v5

--- a/solution.py
+++ b/solution.py
@@ -19,7 +19,7 @@
 SUBS = PARTS // TURNS
 STEP = 16
 OWN, ABOVE, DOWN = 1, 2, 0
-AHEAD = 3
+AHEAD = 4
 DOWN_AHEAD = 2
 LATE_AHEAD = 2
 BETWEEN = 1

time: 61.7 us -> 61.7 us (level)
  no operation moved by 1% of the time
where the time goes in v6:
time: 61.7 us; the launch traced here: 61.5 us
  Pallas kernels  60.9 us (99%)
  local copies, waits for them, and re-layouts  0.66 us (1%)
    pallas_call x1, Pallas kernels, shards(): pl.pallas_call(sweep, out_shape=pltpu.VMEM(rhs.shape, F32), in_specs=[in_...  60.9 us

profile of v6, /device:TPU:7, one launch (start us, length us, event | category | flops | bytes accessed | tf_op | source)
XLA Modules:
  0.0 61.5 jit_solution(12639093322069400735)
XLA Ops:
  0.0 60.9 %sweep.1 = f32[1,16,16,128]{3,2,1,0:T(8,128)S(1)} custom-call(bf16[1,16,16,128]{3,2,1,0:T(8,128)(2,1)} %x_hbm.1, f32[1,16,16,128]{3,2,1,0:T(8,128)} %rhs_hbm.1, bf16[1,16,6,128,128]{4,3,2,1,0:T(8,128)(2,1)} %down_hbm.1, bf16[1,16,6,128,128]{4,3,2,1,0:T(8,128)(2,1)} %level_hbm.1, bf16[1,16,6,128,128]{4,3,2,1,0:T(8,128)(2,1)} %up_hbm.1, ...), custom_call_target="tpu_custom_call" | custom-call | tf_op jit(solution)/shard_map/sweep/pallas_call | solution.py:397
  60.9 0.7 %copy.10 = f32[1,16,16,128]{3,2,1,0:T(8,128)} copy(f32[1,16,16,128]{3,2,1,0:T(8,128)S(1)} %sweep.1) | data formatting | bytes 262144
